TPU v7x, 128 devices: a whole 4x4x4 slice. The times are simulated.
128 devices in a mesh: tm: 32 (over x, z_hi, y), space: 4 (over z_lo, core).
Axes of the slice: x: 4, y: 4, z: 4 (z_hi: 2, z_lo: 2; z = z_hi * 2 + z_lo), core: 2. Of those that a mesh axis runs over, the one named last changes fastest.
Arguments:
- snapshots: bfloat16 [8192, 32768], P('space', 'tm'), may hold values from -6 to 6
Outputs:
- hankel: float32 [32768, 5, 1024], P(('tm', 'space'))
All inputs are finite; a program needn't handle non-finite values.
Results may differ from a plain program's by a relative error of at most 0.0003.
Values may be sent and summed in bfloat16 or wider, within the bound.
A program may use at most 128 MiB of HBM per device.

v0:
```python
import math

import jax
import jax.numpy as jnp
from jax import lax
from jax.sharding import PartitionSpec as P

DELAY = 8
ROUNDS = 4


def shifted(value, axis, by):
    devices = lax.axis_size(axis)
    pairs = [(i, i + by) for i in range(devices) if 0 <= i + by < devices]
    return lax.ppermute(value, axis, pairs)


def shifted_2(value, axis, steps):
    count = lax.axis_size(axis)
    pairs = [(source, (source + steps) % count) for source in range(count)]
    return lax.ppermute(value, axis, pairs)


def tile_of(left, right, width):
    gram = lax.dot_general(
        left, right, (((0,), (0,)), ((), ())), preferred_element_type=jnp.float32
    )
    total = jnp.zeros((width, width), jnp.float32)
    for shift_k in range(DELAY):
        total = total + gram[shift_k : shift_k + width, shift_k : shift_k + width]
    return total


def body(snapshots):
    width = snapshots.shape[1]
    cell_rows = snapshots.shape[0]
    scale_factor = 1.0 / math.sqrt(DELAY * cell_rows * lax.axis_size("space"))
    head = snapshots[:, : DELAY - 1]
    following = shifted(head, "tm", -1)
    extended = jnp.concatenate([snapshots, following], axis=1)
    tiles = [tile_of(extended, extended, width)]
    moving = extended
    for offset in range(1, ROUNDS + 1):
        moving = shifted_2(moving, "tm", 1)
        tiles.append(tile_of(extended, moving, width))
    stacked = jnp.stack(tiles, axis=1)
    summed = lax.psum_scatter(stacked, "space", scatter_dimension=0, tiled=True)
    return summed * scale_factor


def solution(mesh):
    return jax.shard_map(
        body,
        mesh=mesh,
        in_specs=(P("space", "tm"),),
        out_specs=P(("tm", "space"), None, None),
        check_vma=False,
    )
```

profile of v0, /device:TPU:1, one launch (start us, length us, event | category | flops | bytes accessed | tf_op | source)
XLA Modules:
  0.0 619.4 jit_solution(3042734265814379732)
XLA Ops:
  6.5 6.5 %copy.3 = bf16[2048,1024]{0,1:T(8,128)(2,1)} copy(bf16[2048,1024]{1,0:T(8,128)(2,1)} %param.1) | data formatting | bytes 8388608 | tf_op args[0]
  13.0 0.8 slice.164
  13.8 1.5 collective-permute-start
  15.3 4.0 collective-permute-done
  19.4 2.5 pad_maximum_fusion
  21.9 1.5 collective-permute-start.1
  23.4 95.1 %collective-permute-done.1 = bf16[2048,1031]{0,1:T(8,128)(2,1)S(1)} collective-permute-done((bf16[2048,1031]{0,1:T(8,128)(2,1)S(1)}, bf16[2048,1031]{0,1:T(8,128)(2,1)S(1)}, u32[]{:S(2)}, u32[]{:S(2)}) %collective-permute-start.1) | collective-permute-done | bytes 4223008 | tf_op jit(solution)/shard_map/ppermute | solution.py:21
  118.5 0.0 collective-permute-start.2
  118.5 95.8 %collective-permute-done.2 = bf16[2048,1031]{0,1:T(8,128)(2,1)} collective-permute-done((bf16[2048,1031]{0,1:T(8,128)(2,1)S(1)}, bf16[2048,1031]{0,1:T(8,128)(2,1)}, u32[]{:S(2)}, u32[]{:S(2)}) %collective-permute-start.2) | collective-permute-done | bytes 4223008 | tf_op jit(solution)/shard_map/ppermute | solution.py:21
  214.3 5.7 fusion.14
  220.1 9.0 %fusion.9 = f32[1024,5,1024]{2,0,1:T(8,128)} fusion(f32[1031,1031]{1,0:T(8,128)S(1)} %fusion.14), kind=kLoop, calls=%fused_computation.39 | loop fusion | flops 7340031 | bytes 37748736
  229.1 8.0 %fusion.13 = f32[1031,1031]{1,0:T(8,128)S(1)} fusion(bf16[2048,1031]{0,1:T(8,128)(2,1)} %copy-done.1, bf16[2048,7]{0,1:T(8,128)(2,1)S(1)} %collective-permute-done, bf16[2048,1024]{0,1:T(8,128)(2,1)S(1)} %copy-done), kind=kOutput, calls=%fused_computation.50 | convolution fusion | flops 4362334208 | bytes 12697796 | tf_op jit(solution)/shard_map/dot_general | solution.py:25
  237.1 11.8 %fusion.7 = f32[1024,5,1024]{2,0,1:T(8,128)} fusion(f32[1024,5,1024]{2,0,1:T(8,128)} %fusion.9, f32[1031,1031]{1,0:T(8,128)S(1)} %fusion.13), kind=kLoop, calls=%fused_computation.30 | loop fusion | flops 7340032 | bytes 37748736
  248.9 60.4 %collective-permute-done.3 = bf16[2048,1031]{0,1:T(8,128)(2,1)S(1)} collective-permute-done((bf16[2048,1031]{0,1:T(8,128)(2,1)}, bf16[2048,1031]{0,1:T(8,128)(2,1)S(1)}, u32[]{:S(2)}, u32[]{:S(2)}) %collective-permute-start.3) | collective-permute-done | bytes 4223008 | tf_op jit(solution)/shard_map/ppermute | solution.py:21
  309.3 8.0 %fusion.12 = f32[1031,1031]{1,0:T(8,128)S(1)} fusion(bf16[2048,1031]{0,1:T(8,128)(2,1)} %collective-permute-done.2, bf16[2048,7]{0,1:T(8,128)(2,1)S(1)} %collective-permute-done, bf16[2048,1024]{0,1:T(8,128)(2,1)S(1)} %copy-done), kind=kOutput, calls=%fused_computation.49 | convolution fusion | flops 4362334208 | bytes 12697796 | tf_op jit(solution)/shard_map/dot_general | solution.py:25
  317.3 11.9 %fusion.5 = f32[1024,5,1024]{2,0,1:T(8,128)} fusion(f32[1024,5,1024]{2,0,1:T(8,128)} %fusion.7, f32[1031,1031]{1,0:T(8,128)S(1)} %fusion.12), kind=kLoop, calls=%fused_computation.21 | loop fusion | flops 7340032 | bytes 37748736
  329.2 5.7 fusion.11
  335.0 11.7 %fusion.3 = f32[1024,5,1024]{2,0,1:T(8,128)} fusion(f32[1024,5,1024]{2,0,1:T(8,128)} %fusion.5, f32[1031,1031]{1,0:T(8,128)S(1)} %fusion.11), kind=kLoop, calls=%fused_computation.12 | loop fusion | flops 7340032 | bytes 37748736
  346.7 56.6 %collective-permute-done.4 = bf16[2048,1031]{0,1:T(8,128)(2,1)} collective-permute-done((bf16[2048,1031]{0,1:T(8,128)(2,1)S(1)}, bf16[2048,1031]{0,1:T(8,128)(2,1)}, u32[]{:S(2)}, u32[]{:S(2)}) %collective-permute-start.4) | collective-permute-done | bytes 4223008 | tf_op jit(solution)/shard_map/ppermute | solution.py:21
  403.2 8.0 %fusion.10 = f32[1031,1031]{1,0:T(8,128)S(1)} fusion(bf16[2048,1031]{0,1:T(8,128)(2,1)} %collective-permute-done.4, bf16[2048,7]{0,1:T(8,128)(2,1)S(1)} %collective-permute-done, bf16[2048,1024]{0,1:T(8,128)(2,1)S(1)} %copy-done), kind=kOutput, calls=%fused_computation.47 | convolution fusion | flops 4362334208 | bytes 12697796 | tf_op jit(solution)/shard_map/dot_general | solution.py:25
  411.2 11.7 %fusion.1 = f32[1024,5,1024]{2,0,1:T(8,128)} fusion(f32[1024,5,1024]{2,0,1:T(8,128)} %fusion.3, f32[1031,1031]{1,0:T(8,128)S(1)} %fusion.10), kind=kLoop, calls=%fused_computation.3 | loop fusion | flops 7340032 | bytes 37748736 | tf_op jit(solution)/shard_map/stack | solution.py:46
  423.0 0.0 reduce-scatter.2.cloned.1.call-update
  423.0 183.4 %reduce-scatter.2.cloned.1.call-done = f32[256,5,1024]{2,0,1:T(8,128)} async-done(((f32[1024,5,1024]{2,0,1:T(8,128)}), f32[256,5,1024]{2,0,1:T(8,128)}) %reduce-scatter.2.cloned.1.call-update) | async-done | bytes 5242896 | tf_op jit(solution)/shard_map/reduce_scatter | solution.py:47
  606.4 6.0 broadcast_multiply_fusion
  (7 shorter events, 0.0 us)
Async XLA Ops:
  6.5 599.8 %reduce-scatter.2.cloned.1.call-start = ((), (), s32[]{:S(2)}) async-start(), calls=%async_computation.1 | async-start | bytes 26214400 | tf_op jit(solution)/shard_map/reduce_scatter | solution.py:47
  13.8 200.6 %copy-start = (bf16[2048,1024]{0,1:T(8,128)(2,1)S(1)}, bf16[2048,1024]{0,1:T(8,128)(2,1)}, u32[]{:S(2)}) copy-start(bf16[2048,1024]{0,1:T(8,128)(2,1)} %copy.3) | copy-start | bytes 12582916
  13.8 5.6 collective-permute-start
  21.9 96.7 %collective-permute-start.1 = (bf16[2048,1031]{0,1:T(8,128)(2,1)S(1)}, bf16[2048,1031]{0,1:T(8,128)(2,1)S(1)}, u32[]{:S(2)}, u32[]{:S(2)}) collective-permute-start(bf16[2048,1031]{0,1:T(8,128)(2,1)S(1)} %pad_maximum_fusion), channel_id=1, source_target_pairs={{0,4},{4,8},{8,12},{12,16},{16,20},{20,24},{24,28},{28,32},{32,36}... | collective-permute-start | bytes 12668936 | tf_op jit(solution)/shard_map/ppermute | solution.py:21
  118.5 95.8 %copy-start.1 = (bf16[2048,1031]{0,1:T(8,128)(2,1)}, bf16[2048,1031]{0,1:T(8,128)(2,1)S(1)}, u32[]{:S(2)}) copy-start(bf16[2048,1031]{0,1:T(8,128)(2,1)S(1)} %collective-permute-done.1) | copy-start | bytes 12668932
  118.5 95.8 %collective-permute-start.2 = (bf16[2048,1031]{0,1:T(8,128)(2,1)S(1)}, bf16[2048,1031]{0,1:T(8,128)(2,1)}, u32[]{:S(2)}, u32[]{:S(2)}) collective-permute-start(bf16[2048,1031]{0,1:T(8,128)(2,1)S(1)} %collective-permute-done.1), channel_id=1, source_target_pairs={{0,4},{4,8},{8,12},{12,16},{16,20},{20,24},{24,28},{28,32},{32,36}... | collective-permute-start | bytes 12668936 | tf_op jit(solution)/shard_map/ppermute | solution.py:21
  214.3 95.0 %collective-permute-start.3 = (bf16[2048,1031]{0,1:T(8,128)(2,1)}, bf16[2048,1031]{0,1:T(8,128)(2,1)S(1)}, u32[]{:S(2)}, u32[]{:S(2)}) collective-permute-start(bf16[2048,1031]{0,1:T(8,128)(2,1)} %collective-permute-done.2), channel_id=1, source_target_pairs={{0,4},{4,8},{8,12},{12,16},{16,20},{20,24},{24,28},{28,32},{32,36}... | collective-permute-start | bytes 12668936 | tf_op jit(solution)/shard_map/ppermute | solution.py:21
  309.3 93.9 %collective-permute-start.4 = (bf16[2048,1031]{0,1:T(8,128)(2,1)S(1)}, bf16[2048,1031]{0,1:T(8,128)(2,1)}, u32[]{:S(2)}, u32[]{:S(2)}) collective-permute-start(bf16[2048,1031]{0,1:T(8,128)(2,1)S(1)} %collective-permute-done.3), channel_id=1, source_target_pairs={{0,4},{4,8},{8,12},{12,16},{16,20},{20,24},{24,28},{28,32},{32,36}... | collective-permute-start | bytes 12668936 | tf_op jit(solution)/shard_map/ppermute | solution.py:21
Sparse Core Ops, SparseCore 0:
  423.1 183.2 reduce-scatter.1
where the time goes:
time: 629 us; the launch traced here: 619 us
  waiting for transfers between devices  495 us (79%)
  other arithmetic  64.6 us (10%)
  matrix products  35.5 us (6%)
  between operations  13.7 us (2%)
  local copies, waits for them, and re-layouts  7.25 us (1%)
    ppermute x4, waiting for transfers between devices, shifted_2(): return lax.ppermute(value, axis, pairs)  308 us
    reduce_scatter x1, waiting for transfers between devices, body(): summed = lax.psum_scatter(stacked, 'space', scatter_dimension=0, tiled=True)  183 us
    unnamed x4, other arithmetic  44.4 us
    dot_general x5, matrix products, tile_of(): lax.dot_general(left, right, (((0,), (0,)), ((), ())), preferred_element_...  35.5 us
  transfers between devices with their start and end apart: 6, of which 6 were waited for; matrix products, arithmetic and copies ran while one was open for 12% of the time, Pallas kernels for 0%

commit v1 on v0

v1 whole, which is shorter than its diff:
```python
import functools
import math

import jax
import jax.numpy as jnp
from jax import lax
from jax.experimental import pallas as pl
from jax.experimental.pallas import tpu as pltpu
from jax.sharding import PartitionSpec as P

DELAY = 8
PAIRS = 5
CHUNKS = 4
HEAD = 16
POWER = 14.0
TOP = 125.0 * math.log(2.0)
MESH = pl.DeviceIdType.MESH
ORDER = [
    (4, 0), (1, 0), (3, 0), (0, 0), 4,
    (4, 1), (1, 1), (0, 1), (3, 1), 5,
    (0, 2), (0, 3), (4, 2), 6,
    (1, 2), (3, 2), 7,
    (4, 3), (1, 3), (2, 0), (2, 1), (2, 2), (3, 3), (2, 3),
]
TASKS = [entry for entry in ORDER if isinstance(entry, tuple)]
STAGES = 3


def encode(value):
    top = jnp.max(jnp.abs(value), axis=0, keepdims=True)
    top = jnp.maximum(top, 1e-35).astype(jnp.bfloat16)
    ratio = jnp.abs(value) / top.astype(jnp.float32)
    code = jnp.exp(POWER * jnp.log(jnp.maximum(ratio, 1e-30)) + TOP)
    code = jnp.where(value < 0.0, -code, code).astype(jnp.bfloat16)
    return code, jnp.broadcast_to(top, (HEAD, value.shape[1]))


def decode(code, top):
    code = code.astype(jnp.float32)
    size = jnp.exp((jnp.log(jnp.maximum(jnp.abs(code), 1e-37)) - TOP) * (1.0 / POWER))
    size = size * top.astype(jnp.float32)
    return jnp.where(code == 0.0, 0.0, jnp.where(code < 0.0, -size, size))


def kernel(
    count, scale, x_ref, out_ref,
    buf, at, hb, hx, hn, halo, stage, inbox, zout, zin, acc, rout, rin,
    local_sem, swap_s, swap_r, cross_s, cross_r, plus_s, plus_r, minus_s, minus_r,
    hswap_s, hswap_r, head_s, head_r, core_s, core_r, z_s, z_r, back_s, back_r, out_sem,
):
    cells, width = x_ref.shape
    half = cells // 2
    chunk = width // CHUNKS
    strip = width // 4
    rows = strip + HEAD
    lane = halo.shape[-1]

    t = lax.axis_index("tm")
    s = lax.axis_index("space")
    y = lax.rem(t, 4)
    base = t - y
    zh = lax.rem(lax.div(t, 4), 2)
    zlo = lax.div(s, 2)
    core = lax.rem(s, 2)
    flip = (1 - zlo) * 2 + core
    keep = pl.multiple_of(zh * half, half)
    away = pl.multiple_of((1 - zh) * half, half)

    def block(steps):
        return lax.rem(t + steps + count, count)

    def aligned(steps):
        there = block(steps)
        other = lax.rem(lax.div(there, 4), 2)
        return there, lax.select(other == zh, s, flip)

    partner = (t, flip)
    sibling = (t, zlo * 2 + 1 - core)
    above = (base + lax.rem(y + 1, 4), s)
    below = (base + lax.rem(y + 3, 4), s)
    onward = (block(4), flip)
    heads_to = [aligned(-1), aligned(2), aligned(3)]
    home = (block(-1), s)

    barrier = pltpu.get_barrier_semaphore()
    greet = [partner, sibling, above, below, onward, (block(-4), flip)]
    greet += heads_to + [aligned(1), aligned(-2), aligned(-3)]
    greet += [home, (block(1), s)]
    for device in greet:
        pl.semaphore_signal(barrier, inc=1, device_id=device, device_id_type=MESH)
    pl.semaphore_wait(barrier, len(greet))

    def remote(src, dst, send, recv, device):
        return pltpu.make_async_remote_copy(
            src_ref=src, dst_ref=dst, send_sem=send, recv_sem=recv,
            device_id=device, device_id_type=MESH,
        )

    def local(n):
        q = CHUNKS - 1 - n
        return pltpu.make_async_copy(
            x_ref.at[pl.ds(keep, half), q * chunk : (q + 1) * chunk],
            buf.at[0, q, pl.ds(keep, half), :],
            local_sem.at[n],
        )

    def swap(n):
        q = CHUNKS - 1 - n
        return remote(
            x_ref.at[pl.ds(away, half), q * chunk : (q + 1) * chunk],
            buf.at[0, q, pl.ds(away, half), :],
            swap_s.at[n], swap_r.at[n], partner,
        )

    def stream(n, phase, source, target, off, send, recv, device):
        q = CHUNKS - 1 - n
        return remote(
            buf.at[source, q, pl.ds(off, half), :],
            buf.at[target, q, pl.ds(off, half), :],
            send.at[n, phase], recv.at[n, phase], device,
        )

    def cross(n, phase):
        off = keep if phase == 0 else away
        return stream(n, phase, 0, 3, off, cross_s, cross_r, onward)

    def plus(n, phase, source, off):
        return stream(n, phase, source, 1, off, plus_s, plus_r, above)

    def minus(n, phase, source, off):
        return stream(n, phase, source, 2, off, minus_s, minus_r, below)

    def own_ready(n, phase):
        off = keep if phase == 0 else away
        cross(n, phase).start()

        @pl.when(y < 3)
        def _():
            plus(n, phase, 0, off).start()

        @pl.when(y == 0)
        def _():
            minus(n, phase, 0, off).start()

    def cross_ready(index):
        n, phase = index // 2, index % 2
        off = away if phase == 0 else keep
        cross(n, phase).wait_recv()

        @pl.when(y == 3)
        def _():
            plus(n, phase, 3, off).start()

        @pl.when(y > 0)
        def _():
            minus(n, phase, 3, off).start()

    def transpose(which, source, n):
        q = CHUNKS - 1 - n

        @pl.loop(0, cells // strip)
        def _(i):
            at_cell = pl.multiple_of(i * strip, strip)
            at[which, q * chunk : (q + 1) * chunk, pl.ds(at_cell, strip)] = buf[
                source, q, pl.ds(at_cell, strip), :
            ].T

    head_copy = pltpu.make_async_copy(x_ref.at[:, 0:lane], hx, local_sem.at[CHUNKS])
    head_copy.start()
    for n in range(CHUNKS):
        local(n).start()
    for n in range(CHUNKS):
        swap(n).start()

    local(0).wait()
    own_ready(0, 0)

    head_copy.wait()

    @pl.loop(0, cells // strip)
    def _(i):
        at_cell = pl.multiple_of(i * strip, strip)
        piece = hx[pl.ds(at_cell, strip), :].T[0:HEAD]
        hn[:, pl.ds(at_cell, strip)] = jnp.where(t == 0, jnp.zeros_like(piece), piece)

    hb[1, :, pl.ds(keep, half)] = hn[:, pl.ds(keep, half)]
    head_swap = remote(
        hn.at[:, pl.ds(away, half)], hb.at[1, :, pl.ds(away, half)],
        hswap_s, hswap_r, partner,
    )
    head_swap.start()
    head_swap.wait_recv()
    heads = [
        remote(hb.at[1], hb.at[slot], head_s.at[i], head_r.at[i], device)
        for i, (slot, device) in enumerate(zip((0, 2, 3), heads_to))
    ]
    for copy in heads:
        copy.start()
    at[1, width : width + HEAD, :] = hb[1]

    for n in range(CHUNKS):
        swap(n).wait_recv()
        own_ready(n, 1)
        if n + 1 < CHUNKS:
            local(n + 1).wait()
            own_ready(n + 1, 0)
        if n == 0:
            for copy in heads:
                copy.wait_recv()
            at[0, width : width + HEAD, :] = hb[0]
        transpose(0, 0, n)
        cross_ready(n)

    def core_copy(k):
        return remote(
            stage.at[k % STAGES, 1 - core], inbox.at[k],
            core_s.at[k], core_r.at[k], sibling,
        )

    def z_copy(k):
        return remote(zout.at[k], zin.at[k], z_s.at[k], z_r.at[k], partner)

    def back_copy(n):
        return remote(rout.at[n], rin.at[n], back_s.at[n], back_r.at[n], home)

    def out_copy(k):
        r, n = TASKS[k]
        q = CHUNKS - 1 - n
        return pltpu.make_async_copy(
            acc.at[k], out_ref.at[r, :, q * chunk : (q + 1) * chunk], out_sem.at[k]
        )

    def compute(k):
        r, n = TASKS[k]
        q = CHUNKS - 1 - n
        left = 1 if r == 2 else 0
        right = (0, 1, 2, 2, 3)[r]
        if k >= STAGES:
            core_copy(k - STAGES).wait_send()

        @pl.loop(0, 4)
        def _(p):
            lhs = at[left, pl.ds(pl.multiple_of(p * strip, strip), rows), :]
            gram = jnp.dot(lhs, buf[right, q], preferred_element_type=jnp.float32)
            if n == 0:
                after = lax.dot_general(
                    lhs, hb[right], (((1,), (1,)), ((), ())),
                    preferred_element_type=jnp.float32,
                )
                halo[r, p, :, 0:HEAD] = after
            full = jnp.concatenate([gram, halo[r, p]], axis=1)
            halo[r, p] = gram[:, 0:lane]
            by = 1
            while by < DELAY:
                moved = pltpu.roll(full, rows - by, 0)
                full = full + pltpu.roll(moved, chunk + lane - by, 1)
                by *= 2
            stage[k % STAGES, lax.rem(p, 2), lax.div(p, 2)] = (
                full[0:strip, 0:chunk] * scale
            )

        core_copy(k).start()

    def send_z(k):
        core_copy(k).wait_recv()
        slot = k % STAGES
        acc[k] = stage[slot, core, zlo] + inbox[k, zlo]
        code, top = encode(stage[slot, core, 1 - zlo] + inbox[k, 1 - zlo])
        zout[k, 0:strip] = code
        zout[k, strip:rows] = top
        z_copy(k).start()

    def finish(k):
        r, n = TASKS[k]
        z_copy(k).wait_recv()
        total = acc[k] + decode(zin[k, 0:strip], zin[k, strip : strip + 1])
        if r == 2:
            code, top = encode(total)
            rout[n, 0:strip] = code
            rout[n, strip:rows] = top
            back_copy(n).start()
        else:
            acc[k] = total
            out_copy(k).start()

    def block_ready(n, kind):
        for phase in range(2):
            kind(n, phase, 0, keep).wait_recv()

    k = 0
    for entry in ORDER:
        if not isinstance(entry, tuple):
            cross_ready(entry)
            continue
        r, n = entry
        if r == 1:
            block_ready(n, plus)
            transpose(1, 1, n)
        if r == 3:
            block_ready(n, minus)
        compute(k)
        if k >= 1:
            send_z(k - 1)
        if k >= 3:
            finish(k - 3)
        k += 1
    send_z(k - 1)
    for j in range(k - 3, k):
        finish(j)
    for j, (r, n) in enumerate(TASKS):
        if r == 2:
            back_copy(n).wait_recv()
            acc[j] = decode(rin[n, 0:strip], rin[n, strip : strip + 1])
            out_copy(j).start()

    for n in range(CHUNKS):
        swap(n).wait_send()
        back_copy(n).wait_send()
        for phase in range(2):
            cross(n, phase).wait_send()
            plus(n, phase, 0, keep).wait_send()
            minus(n, phase, 0, keep).wait_send()
    head_swap.wait_send()
    for copy in heads:
        copy.wait_send()
    for j in range(k):
        if j >= k - STAGES:
            core_copy(j).wait_send()
        z_copy(j).wait_send()
        out_copy(j).wait()


def body(snapshots):
    cells, width = snapshots.shape
    count = lax.axis_size("tm")
    scale = 1.0 / math.sqrt(DELAY * cells * lax.axis_size("space"))
    strip, chunk, half = width // 4, width // CHUNKS, cells // 2
    rows = strip + HEAD
    lane = 128
    tasks = len(TASKS)
    dma = pltpu.SemaphoreType.DMA
    f32, bf16 = jnp.float32, jnp.bfloat16
    out = pl.pallas_call(
        functools.partial(kernel, count, scale),
        out_shape=jax.ShapeDtypeStruct((PAIRS, strip, width), f32),
        in_specs=[pl.BlockSpec(memory_space=pl.ANY)],
        out_specs=pl.BlockSpec(memory_space=pl.ANY),
        scratch_shapes=[
            pltpu.VMEM((4, CHUNKS, cells, chunk), bf16),
            pltpu.VMEM((2, width + HEAD, cells), bf16),
            pltpu.VMEM((4, HEAD, cells), bf16),
            pltpu.VMEM((cells, lane), bf16),
            pltpu.VMEM((HEAD, cells), bf16),
            pltpu.VMEM((PAIRS, 4, rows, lane), f32),
            pltpu.VMEM((STAGES, 2, 2, strip, chunk), f32),
            pltpu.VMEM((tasks, 2, strip, chunk), f32),
            pltpu.VMEM((tasks, rows, chunk), bf16),
            pltpu.VMEM((tasks, rows, chunk), bf16),
            pltpu.VMEM((tasks, strip, chunk), f32),
            pltpu.VMEM((CHUNKS, rows, chunk), bf16),
            pltpu.VMEM((CHUNKS, rows, chunk), bf16),
            dma((CHUNKS + 1,)),
            dma((CHUNKS,)), dma((CHUNKS,)),
            dma((CHUNKS, 2)), dma((CHUNKS, 2)),
            dma((CHUNKS, 2)), dma((CHUNKS, 2)),
            dma((CHUNKS, 2)), dma((CHUNKS, 2)),
            dma, dma,
            dma((3,)), dma((3,)),
            dma((tasks,)), dma((tasks,)),
            dma((tasks,)), dma((tasks,)),
            dma((CHUNKS,)), dma((CHUNKS,)),
            dma((tasks,)),
        ],
        compiler_params=pltpu.CompilerParams(
            collective_id=0, has_side_effects=True, vmem_limit_bytes=60 * 2**20
        ),
        cost_estimate=pl.CostEstimate(
            flops=2 * PAIRS * width * width * cells,
            bytes_accessed=2 * cells * width + 4 * PAIRS * strip * width,
            transcendentals=0,
        ),
    )(snapshots)
    return jnp.transpose(out, (1, 0, 2))


def solution(mesh):
    return jax.shard_map(
        body,
        mesh=mesh,
        in_specs=(P("space", "tm"),),
        out_specs=P(("tm", "space"), None, None),
        check_vma=False,
    )
```

time: 629 us -> 202 us (0.32); the launches traced: 619 us -> 201 us
  waiting for transfers between devices: 495 us -> 0 us
  Pallas kernels: 0 us -> 195 us
  other arithmetic: 64.6 us -> 0 us
  matrix products: 35.5 us -> 0 us
  between operations: 13.7 us -> 0.01 us
    ppermute x5 -> x0, waiting for transfers between devices: 312 us -> none  [the longest x4 308 us: shifted_2(): return lax.ppermute(value, axis, pairs)]
    pallas_call x0 -> x1, Pallas kernels: none -> 195 us  [body(): pl.pallas_call(functools.partial(kernel, count, scale), out_shape=jax.Sha...]
    reduce_scatter x1 -> x0, waiting for transfers between devices: 183 us -> none  [body(): summed = lax.psum_scatter(stacked, 'space', scatter_dimension=0, tiled=True)]
    unnamed x4 -> x0, other arithmetic: 44.4 us -> none
    dot_general x5 -> x0, matrix products: 35.5 us -> none  [tile_of(): lax.dot_general(left, right, (((0,), (0,)), ((), ())), preferred_element_...]
    another operation x1 -> x0, other arithmetic: 11.7 us -> none  [body(): stacked = jnp.stack(tiles, axis=1)]
  transfers between devices with their start and end apart: 6 -> 0, of which waited for: 6 -> 0; matrix products, arithmetic and copies ran while one was open for 12% -> 0% of each run, Pallas kernels for 0% -> 0%
where the time goes in v1:
time: 202 us; the launch traced here: 201 us
  Pallas kernels  195 us (97%)
  local copies, waits for them, and re-layouts  5.7 us (3%)
    pallas_call x1, Pallas kernels, body(): pl.pallas_call(functools.partial(kernel, count, scale), out_shape=jax.Sha...  195 us
    unnamed x1, local copies, waits for them, and re-layouts  5.7 us

profile of v1, /device:TPU:1, one launch (start us, length us, event | category | flops | bytes accessed | tf_op | source)
XLA Modules:
  0.0 200.7 jit_solution(11067318475849206589)
XLA Ops:
  0.0 195.0 %shard_map.17 = f32[5,256,1024]{2,1,0:T(8,128)} custom-call(bf16[2048,1024]{1,0:T(8,128)(2,1)} %x_ref.1), custom_call_target="tpu_custom_call" | custom-call | flops 21474836480 | bytes 9437184 | tf_op jit(solution)/shard_map/pallas_call | solution.py:343
  195.0 5.7 %copy.3 = f32[256,5,1024]{2,0,1:T(8,128)} copy(f32[256,5,1024]{2,0,1:T(8,128)} %bitcast.1) | data formatting | bytes 10485760

commit v2 on v1

v2 whole, which is shorter than its diff:
```python
import functools
import math

import jax
import jax.numpy as jnp
from jax import lax
from jax.experimental import pallas as pl
from jax.experimental.pallas import tpu as pltpu
from jax.sharding import PartitionSpec as P

DELAY = 8
PAIRS = 5
CHUNKS = 4
HEAD = 16
SPLIT = 2
LIFT = 2.0 ** (125.0 / 16.0)
MESH = pl.DeviceIdType.MESH
ORDER = [
    (0, 0), (4, 0), 8, (0, 1), ("rows", 0), (1, 0), (0, 2), (3, 0), 9,
    (0, 3), (4, 1), ("cols", 0), 10, ("rows", 1), (1, 1), (3, 1), ("cols", 1), 11,
    (4, 2), 12, ("rows", 2), (1, 2), 13, (3, 2), ("cols", 2), 14, 15,
    ("rows", 3), (2, 0), (2, 1), (2, 2), (4, 3), ("cols", 3), (2, 3), (1, 3), (3, 3),
]
LAG = 4
TASKS = [e for e in ORDER if isinstance(e, tuple) and not isinstance(e[0], str)]
STAGES = 3
STAGE_OF = {}
for _k, _e in enumerate(TASKS):
    STAGE_OF[_k] = -1 if _e[0] in (0, 2) else sum(v >= 0 for v in STAGE_OF.values()) % STAGES


def encode(value):
    top = jnp.max(jnp.abs(value), axis=0, keepdims=True)
    top = jnp.maximum(top, 1e-35).astype(jnp.bfloat16)
    code = value * (LIFT / top.astype(jnp.float32))
    for _ in range(4):
        code = code * code
    code = jnp.where(value < 0.0, -code, code).astype(jnp.bfloat16)
    return code, jnp.broadcast_to(top, (HEAD, value.shape[1]))


def decode(code, top):
    code = code.astype(jnp.float32)
    size = jnp.abs(code)
    for _ in range(4):
        size = lax.rsqrt(size)
    size = size * (top.astype(jnp.float32) * (1.0 / LIFT))
    size = jnp.where(code == 0.0, 0.0, size)
    return jnp.where(code < 0.0, -size, size)


def kernel(
    count, scale, x_ref, out_ref,
    buf, at, hb, hx, hn, saved_one, saved_two, held, stage, inbox, zout, zin, rout, rin,
    local_sem, swap_s, swap_r, cross_s, cross_r, plus_s, plus_r, minus_s, minus_r,
    hswap_s, hswap_r, head_s, head_r, core_s, core_r, z_s, z_r, back_s, back_r, out_sem,
):
    cells, width = x_ref.shape
    half = cells // 2
    chunk = width // CHUNKS
    strip = width // 4
    rows = strip + HEAD
    lane = saved_one.shape[-1]
    piece = half // SPLIT

    t = lax.axis_index("tm")
    s = lax.axis_index("space")
    y = lax.rem(t, 4)
    base = t - y
    zh = lax.rem(lax.div(t, 4), 2)
    zlo = lax.div(s, 2)
    core = lax.rem(s, 2)
    flip = (1 - zlo) * 2 + core
    keep = pl.multiple_of(zh * half, half)
    away = pl.multiple_of((1 - zh) * half, half)

    def block(steps):
        return lax.rem(t + steps + count, count)

    def aligned(steps):
        there = block(steps)
        other = lax.rem(lax.div(there, 4), 2)
        return there, lax.select(other == zh, s, flip)

    partner = (t, flip)
    sibling = (t, zlo * 2 + 1 - core)
    above = (base + lax.rem(y + 1, 4), s)
    below = (base + lax.rem(y + 3, 4), s)
    onward = (block(4), flip)
    heads_to = [aligned(-1), aligned(2), aligned(3)]
    home = (block(-1), s)

    barrier = pltpu.get_barrier_semaphore()
    greet = [partner, sibling, above, below, onward, (block(-4), flip)]
    greet += heads_to + [aligned(1), aligned(-2), aligned(-3)]
    greet += [home, (block(1), s)]
    for device in greet:
        pl.semaphore_signal(barrier, inc=1, device_id=device, device_id_type=MESH)
    pl.semaphore_wait(barrier, len(greet))

    def remote(src, dst, send, recv, device):
        return pltpu.make_async_remote_copy(
            src_ref=src, dst_ref=dst, send_sem=send, recv_sem=recv,
            device_id=device, device_id_type=MESH,
        )

    def local(n):
        q = CHUNKS - 1 - n
        return pltpu.make_async_copy(
            x_ref.at[pl.ds(keep, half), q * chunk : (q + 1) * chunk],
            buf.at[0, q, pl.ds(keep, half), :],
            local_sem.at[n],
        )

    def swap(n, i):
        q = CHUNKS - 1 - n
        off = pl.multiple_of(away + i * piece, piece)
        return remote(
            x_ref.at[pl.ds(off, piece), q * chunk : (q + 1) * chunk],
            buf.at[0, q, pl.ds(off, piece), :],
            swap_s.at[n, i], swap_r.at[n, i], partner,
        )

    def stream(n, phase, source, target, off, send, recv, device):
        q = CHUNKS - 1 - n
        return remote(
            buf.at[source, q, pl.ds(off, piece), :],
            buf.at[target, q, pl.ds(off, piece), :],
            send.at[n, phase], recv.at[n, phase], device,
        )

    def part(first, second, phase):
        start = first if phase < SPLIT else second
        return pl.multiple_of(start + phase % SPLIT * piece, piece)

    def cross(n, phase):
        off = part(keep, away, phase)
        return stream(n, phase, 0, 3, off, cross_s, cross_r, onward)

    def plus(n, phase, source, off):
        return stream(n, phase, source, 1, off, plus_s, plus_r, above)

    def minus(n, phase, source, off):
        return stream(n, phase, source, 2, off, minus_s, minus_r, below)

    def own_ready(n, phase):
        off = part(keep, away, phase)
        cross(n, phase).start()

        @pl.when(y < 3)
        def _():
            plus(n, phase, 0, off).start()

        @pl.when(y == 0)
        def _():
            minus(n, phase, 0, off).start()

    def cross_ready(index):
        n, phase = index // (2 * SPLIT), index % (2 * SPLIT)
        off = part(away, keep, phase)
        cross(n, phase).wait_recv()

        @pl.when(y == 3)
        def _():
            plus(n, phase, 3, off).start()

        @pl.when(y > 0)
        def _():
            minus(n, phase, 3, off).start()

    def transpose(which, source, n):
        q = CHUNKS - 1 - n

        @pl.loop(0, cells // strip)
        def _(i):
            at_cell = pl.multiple_of(i * strip, strip)
            at[which, q * chunk : (q + 1) * chunk, pl.ds(at_cell, strip)] = buf[
                source, q, pl.ds(at_cell, strip), :
            ].T

    head_copy = pltpu.make_async_copy(x_ref.at[:, 0:lane], hx, local_sem.at[CHUNKS])
    head_copy.start()
    for n in range(CHUNKS):
        local(n).start()
    for i in range(SPLIT):
        swap(0, i).start()

    local(0).wait()
    for phase in range(SPLIT):
        own_ready(0, phase)

    head_copy.wait()

    @pl.loop(0, cells // strip)
    def _(i):
        at_cell = pl.multiple_of(i * strip, strip)
        top = hx[pl.ds(at_cell, strip), :].T[0:HEAD]
        hn[:, pl.ds(at_cell, strip)] = jnp.where(t == 0, jnp.zeros_like(top), top)

    hb[1, :, pl.ds(keep, half)] = hn[:, pl.ds(keep, half)]
    head_swap = remote(
        hn.at[:, pl.ds(away, half)], hb.at[1, :, pl.ds(away, half)],
        hswap_s, hswap_r, partner,
    )
    head_swap.start()
    for n in range(1, CHUNKS):
        for i in range(SPLIT):
            swap(n, i).start()
    heads = [
        remote(hb.at[1], hb.at[slot], head_s.at[i], head_r.at[i], device)
        for i, (slot, device) in enumerate(zip((0, 2, 3), heads_to))
    ]

    def strips_of(r, p, q, first, saved, put):
        left = 1 if r == 2 else 0
        right = (0, 1, 2, 2, 3)[r]
        reach = saved.shape[1]
        deep = reach + HEAD - DELAY
        lhs = at[left, pl.ds(pl.multiple_of(p * strip, strip), deep), :]
        gram = jnp.dot(lhs, buf[right, q], preferred_element_type=jnp.float32)
        place = lax.broadcasted_iota(jnp.int32, (reach, lane), 1)
        cols = [gram[0:reach, i : i + lane] for i in range(0, chunk, lane)]
        if first:
            after = lax.dot_general(
                lhs, hb[right], (((1,), (1,)), ((), ())),
                preferred_element_type=jnp.float32,
            )
            after = jnp.concatenate(
                [after, jnp.zeros((deep, lane - HEAD), jnp.float32)], axis=1
            )[0:reach]

        def shifted(value, by):
            return pltpu.roll(pltpu.roll(value, reach - by, 0), lane - by, 1)

        for step, by in enumerate((1, 2, 4)):
            moved = [shifted(col, by) for col in cols]
            if first:
                last = shifted(after, by)
                after = after + last
            else:
                last = saved[step]
            saved[step] = moved[0]
            inside = place < lane - by
            cols = [
                col + jnp.where(inside, here, following)
                for col, here, following in zip(cols, moved, moved[1:] + [last])
            ]
        for i, col in enumerate(cols):
            for j in range((reach - DELAY) // strip):
                put(p + j, i * lane, col[j * strip : (j + 1) * strip] * scale)

    def held_strip(r, p, q, first):
        def put(p, at_lane, value):
            held[q, lax.rem(p, 2), lax.div(p, 2), :, at_lane : at_lane + lane] = value

        strips_of(r, p, q, first, saved_one.at[r // 2, p], put)

    def rows_of(r, n):
        p = CHUNKS - 1 - n
        if n > 0:
            held_strip(r, p, CHUNKS - 1, True)
        if n > 1:

            @pl.loop(1, n)
            def _(m):
                held_strip(r, p, CHUNKS - 1 - m, False)

    def cols_of(r, n):
        @pl.loop(CHUNKS - 1 - n, CHUNKS)
        def _(p):
            held_strip(r, p, CHUNKS - 1 - n, n == 0)

    def source(k):
        r, n = TASKS[k]
        return held.at[CHUNKS - 1 - n] if r in (0, 2) else stage.at[STAGE_OF[k]]

    def core_copy(k):
        return remote(
            source(k).at[1 - core], inbox.at[k], core_s.at[k], core_r.at[k], sibling
        )

    def compute(k):
        r, n = TASKS[k]
        if r not in (0, 2):
            slot = STAGE_OF[k]
            for j in range(k - 1, -1, -1):
                if STAGE_OF[j] == slot:
                    core_copy(j).wait_send()
                    break

            @pl.loop(0, 2)
            def _(pair):
                def put(p, at_lane, value):
                    stage[
                        slot, lax.rem(p, 2), lax.div(p, 2), :, at_lane : at_lane + lane
                    ] = value

                strips_of(
                    r, pair * 2, CHUNKS - 1 - n, n == 0,
                    saved_two.at[(None, 0, None, 1, 2)[r], pair], put,
                )

        core_copy(k).start()

    for n in range(CHUNKS):
        for i in range(SPLIT):
            swap(n, i).wait_recv()
            own_ready(n, SPLIT + i)
        if n + 1 < CHUNKS:
            local(n + 1).wait()
            for phase in range(SPLIT):
                own_ready(n + 1, phase)
        if n == 0:
            head_swap.wait_recv()
            for copy in heads:
                copy.start()
            at[1, width : width + HEAD, :] = hb[1]
        transpose(0, 0, n)
        for i in range(SPLIT):
            cross_ready(n * SPLIT + i)
        if n == 1:
            for copy in heads:
                copy.wait_recv()
            at[0, width : width + HEAD, :] = hb[0]
            rows_of(0, 0)
            cols_of(0, 0)
        if n >= 1:
            rows_of(0, n)
            cols_of(0, n)

    def z_copy(k):
        return remote(zout.at[k], zin.at[k], z_s.at[k], z_r.at[k], partner)

    def back_copy(n):
        return remote(rout.at[n], rin.at[n], back_s.at[n], back_r.at[n], home)

    def out_copy(k):
        r, n = TASKS[k]
        q = CHUNKS - 1 - n
        return pltpu.make_async_copy(
            inbox.at[k, zlo], out_ref.at[r, :, q * chunk : (q + 1) * chunk], out_sem.at[k]
        )

    def send_z(k):
        core_copy(k).wait_recv()
        own = source(k)
        inbox[k, zlo] = own[core, zlo] + inbox[k, zlo]
        code, top = encode(own[core, 1 - zlo] + inbox[k, 1 - zlo])
        zout[k, 0:strip] = code
        zout[k, strip:rows] = top
        z_copy(k).start()

    def finish(k):
        r, n = TASKS[k]
        z_copy(k).wait_recv()
        total = inbox[k, zlo] + decode(zin[k, 0:strip], zin[k, strip : strip + 1])
        if r == 2:
            code, top = encode(total)
            rout[n, 0:strip] = code
            rout[n, strip:rows] = top
            back_copy(n).start()
        else:
            inbox[k, zlo] = total
            out_copy(k).start()

    def block_ready(n, kind):
        for phase in range(2 * SPLIT):
            kind(n, phase, 0, keep).wait_recv()

    k = 0
    for entry in ORDER:
        if not isinstance(entry, tuple):
            cross_ready(entry)
            continue
        r, n = entry
        if r == "rows":
            block_ready(n, plus)
            transpose(1, 1, n)
            rows_of(2, n)
            continue
        if r == "cols":
            if n == 0:
                for j in range(k):
                    if TASKS[j][0] == 0:
                        core_copy(j).wait_send()
            if n == CHUNKS - 1:
                block_ready(n, minus)
            cols_of(2, n)
            continue
        if r == 3 and n < CHUNKS - 1:
            block_ready(n, minus)
        compute(k)
        if k >= 1:
            send_z(k - 1)
        if k >= LAG:
            finish(k - LAG)
        k += 1
    send_z(k - 1)
    for j in range(k - LAG, k):
        finish(j)
    for j, (r, n) in enumerate(TASKS):
        if r == 2:
            back_copy(n).wait_recv()
            inbox[j, zlo] = decode(rin[n, 0:strip], rin[n, strip : strip + 1])
            out_copy(j).start()

    for n in range(CHUNKS):
        for i in range(SPLIT):
            swap(n, i).wait_send()
        back_copy(n).wait_send()
        for phase in range(2 * SPLIT):
            cross(n, phase).wait_send()
            plus(n, phase, 0, keep).wait_send()
            minus(n, phase, 0, keep).wait_send()
    head_swap.wait_send()
    for copy in heads:
        copy.wait_send()
    for slot in range(STAGES):
        core_copy(max(j for j in range(k) if STAGE_OF[j] == slot)).wait_send()
    for j in range(k):
        if TASKS[j][0] == 2:
            core_copy(j).wait_send()
        z_copy(j).wait_send()
        out_copy(j).wait()


def body(snapshots):
    cells, width = snapshots.shape
    count = lax.axis_size("tm")
    scale = 1.0 / math.sqrt(DELAY * cells * lax.axis_size("space"))
    strip, chunk, half = width // 4, width // CHUNKS, cells // 2
    rows = strip + HEAD
    lane = 128
    tasks = len(TASKS)
    dma = pltpu.SemaphoreType.DMA
    f32, bf16 = jnp.float32, jnp.bfloat16
    out = pl.pallas_call(
        functools.partial(kernel, count, scale),
        out_shape=jax.ShapeDtypeStruct((PAIRS, strip, width), f32),
        in_specs=[pl.BlockSpec(memory_space=pl.ANY)],
        out_specs=pl.BlockSpec(memory_space=pl.ANY),
        scratch_shapes=[
            pltpu.VMEM((4, CHUNKS, cells, chunk), bf16),
            pltpu.VMEM((2, width + HEAD, cells), bf16),
            pltpu.VMEM((4, HEAD, cells), bf16),
            pltpu.VMEM((cells, lane), bf16),
            pltpu.VMEM((HEAD, cells), bf16),
            pltpu.VMEM((2, 4, 3, strip + DELAY, lane), f32),
            pltpu.VMEM((3, 2, 3, 2 * strip + DELAY, lane), f32),
            pltpu.VMEM((CHUNKS, 2, 2, strip, chunk), f32),
            pltpu.VMEM((STAGES, 2, 2, strip, chunk), f32),
            pltpu.VMEM((tasks, 2, strip, chunk), f32),
            pltpu.VMEM((tasks, rows, chunk), bf16),
            pltpu.VMEM((tasks, rows, chunk), bf16),
            pltpu.VMEM((CHUNKS, rows, chunk), bf16),
            pltpu.VMEM((CHUNKS, rows, chunk), bf16),
            dma((CHUNKS + 1,)),
            dma((CHUNKS, SPLIT)), dma((CHUNKS, SPLIT)),
            dma((CHUNKS, 2 * SPLIT)), dma((CHUNKS, 2 * SPLIT)),
            dma((CHUNKS, 2 * SPLIT)), dma((CHUNKS, 2 * SPLIT)),
            dma((CHUNKS, 2 * SPLIT)), dma((CHUNKS, 2 * SPLIT)),
            dma, dma,
            dma((3,)), dma((3,)),
            dma((tasks,)), dma((tasks,)),
            dma((tasks,)), dma((tasks,)),
            dma((CHUNKS,)), dma((CHUNKS,)),
            dma((tasks,)),
        ],
        compiler_params=pltpu.CompilerParams(
            collective_id=0, has_side_effects=True, vmem_limit_bytes=60 * 2**20
        ),
        cost_estimate=pl.CostEstimate(
            flops=2 * PAIRS * width * width * cells,
            bytes_accessed=2 * cells * width + 4 * PAIRS * strip * width,
            transcendentals=0,
        ),
    )(snapshots)
    return jnp.transpose(out, (1, 0, 2))


def solution(mesh):
    return jax.shard_map(
        body,
        mesh=mesh,
        in_specs=(P("space", "tm"),),
        out_specs=P(("tm", "space"), None, None),
        check_vma=False,
    )
```

time: 202 us -> 163 us (0.81)
  Pallas kernels: 195 us -> 157 us
    pallas_call x1, Pallas kernels: 195 us -> 157 us  [body(): pl.pallas_call(functools.partial(kernel, count, scale), out_shape=jax.Sha...]
where the time goes in v2:
time: 163 us
  Pallas kernels  157 us (96%)
  local copies, waits for them, and re-layouts  5.7 us (3%)
    pallas_call x1, Pallas kernels, body(): pl.pallas_call(functools.partial(kernel, count, scale), out_shape=jax.Sha...  157 us
    unnamed x1, local copies, waits for them, and re-layouts  5.7 us

profile of v2, /device:TPU:1, one launch (start us, length us, event | category | flops | bytes accessed | tf_op | source)
XLA Modules:
  0.0 162.9 jit_solution(13752085220143255687)
XLA Ops:
  0.0 157.2 %shard_map.17 = f32[5,256,1024]{2,1,0:T(8,128)} custom-call(bf16[2048,1024]{1,0:T(8,128)(2,1)} %x_ref.1), custom_call_target="tpu_custom_call" | custom-call | flops 21474836480 | bytes 9437184 | tf_op jit(solution)/shard_map/pallas_call | solution.py:437
  157.2 5.7 %copy.3 = f32[256,5,1024]{2,0,1:T(8,128)} copy(f32[256,5,1024]{2,0,1:T(8,128)} %bitcast.1) | data formatting | bytes 10485760

commit v3 on v2

--- a/solution.py
+++ b/solution.py
@@ -19,7 +19,7 @@
     (0, 0), (4, 0), 8, (0, 1), ("rows", 0), (1, 0), (0, 2), (3, 0), 9,
     (0, 3), (4, 1), ("cols", 0), 10, ("rows", 1), (1, 1), (3, 1), ("cols", 1), 11,
     (4, 2), 12, ("rows", 2), (1, 2), 13, (3, 2), ("cols", 2), 14, 15,
-    ("rows", 3), (2, 0), (2, 1), (2, 2), (4, 3), ("cols", 3), (2, 3), (1, 3), (3, 3),
+    (4, 3), ("rows", 3), (2, 0), (2, 1), (2, 2), ("cols", 3), (2, 3), (1, 3), (3, 3),
 ]
 LAG = 4
 TASKS = [e for e in ORDER if isinstance(e, tuple) and not isinstance(e[0], str)]

time: 163 us -> 160 us (0.982)
  Pallas kernels: 157 us -> 154 us
    pallas_call x1, Pallas kernels: 157 us -> 154 us  [body(): pl.pallas_call(functools.partial(kernel, count, scale), out_shape=jax.Sha...]
where the time goes in v3:
time: 160 us
  Pallas kernels  154 us (96%)
  local copies, waits for them, and re-layouts  5.7 us (4%)
    pallas_call x1, Pallas kernels, body(): pl.pallas_call(functools.partial(kernel, count, scale), out_shape=jax.Sha...  154 us
    unnamed x1, local copies, waits for them, and re-layouts  5.7 us

profile of v3, /device:TPU:1, one launch (start us, length us, event | category | flops | bytes accessed | tf_op | source)
XLA Modules:
  0.0 159.9 jit_solution(14940047974212226591)
XLA Ops:
  0.0 154.2 %shard_map.17 = f32[5,256,1024]{2,1,0:T(8,128)} custom-call(bf16[2048,1024]{1,0:T(8,128)(2,1)} %x_ref.1), custom_call_target="tpu_custom_call" | custom-call | flops 21474836480 | bytes 9437184 | tf_op jit(solution)/shard_map/pallas_call | solution.py:437
  154.2 5.7 %copy.3 = f32[256,5,1024]{2,0,1:T(8,128)} copy(f32[256,5,1024]{2,0,1:T(8,128)} %bitcast.1) | data formatting | bytes 10485760
